TPU v7x, 32 devices: a whole 2x2x4 slice. The times are simulated.
32 devices in a mesh: groups: 2 (over y), fsdp: 4 (over z), dp: 2 (over x), pair: 2 (over core).
Axes of the slice: x: 2, y: 2, z: 4, core: 2. Of those that a mesh axis runs over, the one named last changes fastest.
Arguments:
- hidden_input: bfloat16 [4096, 8192], P(('groups', 'fsdp', 'dp', 'pair')), parts along dimension 0, may hold values from -6 to 6
- norm_gain_vector: float32 [8192], replicated, may hold values from 0.5 to 18, as said below
- value_matrix: bfloat16 [8192, 768], P('fsdp'), may hold values from -0.0625 to 0.0625
- adapter_down_map: bfloat16 [16384, 64], P(('groups', 'fsdp')), parts along dimension 0, may hold values from -0.0625 to 0.0625
- adapter_up_map: bfloat16 [128, 768], P('groups'), parts along dimension 0, may hold values from -5 to 5
- values_gradient: bfloat16 [4096, 768], P(('groups', 'fsdp', 'dp', 'pair')), parts along dimension 0, may hold values from -6 to 6
Outputs:
- grad_hidden: bfloat16 [4096, 8192], P(('groups', 'fsdp', 'dp', 'pair')), parts along dimension 0
- grad_down: float32 [16384, 64], P(('groups', 'fsdp')), parts along dimension 0
- grad_up: float32 [128, 768], P('groups'), parts along dimension 0
There are 2 independent parts, one for each index of `groups`. A program takes and returns all parts, laid end to end along the dimension named above; an argument that names none is the same for every part. Nothing has to cross between parts.
Inputs may be any that keep to these rules, and one draw needn't show every extreme that they name: `norm_gain_vector`: positive gains.
All inputs are finite; a program needn't handle non-finite values.
Results may differ from a plain program's by a relative error of at most 0.0085.
Values may be sent and summed in bfloat16 or wider, within the bound.
A program may use at most 64 MiB of HBM per device.

v0:
```python
import math
import jax
import jax.numpy as jnp
from jax import lax
from jax.sharding import PartitionSpec as P

MODEL_WIDTH = 8192
ADAPTER_RANK = 64
norm_eps = 1e-05
adapter_scale = 2.0


def contract_last(left, right):
    return lax.dot_general(
        left, right, (((1,), (1,)), ((), ())), preferred_element_type=jnp.float32
    )


def contract_leading(left, right):
    return lax.dot_general(
        left, right, (((0,), (0,)), ((), ())), preferred_element_type=jnp.float32
    )


def local(
    hidden_input, norm_gain_vector, value_matrix, adapter_down_map, adapter_up_map, values_gradient
):
    width = hidden_input.shape[1]
    stream = hidden_input.astype(jnp.float32)
    inv_rms = lax.rsqrt(jnp.mean(stream * stream, axis=1, keepdims=True) + norm_eps)
    normalized_input = (stream * inv_rms * norm_gain_vector).astype(jnp.bfloat16)
    upward_product = (
        adapter_scale
        * jnp.dot(values_gradient, adapter_up_map.T, preferred_element_type=jnp.float32)
    ).astype(jnp.bfloat16)
    every_values, every_upward = (
        lax.all_gather(values_gradient, "fsdp", axis=0, tiled=True),
        lax.all_gather(upward_product, "fsdp", axis=0, tiled=True),
    )
    columns = contract_last(every_values, value_matrix) + contract_last(
        every_upward, adapter_down_map
    )
    gradient_normalized = lax.all_to_all(
        columns.astype(jnp.bfloat16), "fsdp", split_axis=0, concat_axis=1, tiled=True
    )
    window = normalized_input
    latent_f = jnp.dot(
        window,
        lax.all_gather(adapter_down_map, "fsdp", axis=0, tiled=True),
        preferred_element_type=jnp.float32,
    )
    scaled = gradient_normalized.astype(jnp.float32) * norm_gain_vector
    grad_stream = inv_rms * scaled - stream * (inv_rms**3 / width) * jnp.sum(
        scaled * stream, axis=1, keepdims=True
    )
    latent_code = latent_f.astype(jnp.bfloat16)
    window = normalized_input
    down_shard = lax.psum_scatter(
        contract_leading(window, upward_product), "fsdp", scatter_dimension=0, tiled=True
    )
    up_portion = adapter_scale * contract_leading(latent_code, values_gradient)
    down_shard = lax.psum(down_shard, ("dp", "pair"))
    up_full = lax.psum(up_portion, ("fsdp", "dp", "pair"))
    total = lax.psum(jnp.sum(down_shard * down_shard), "fsdp") + jnp.sum(up_full * up_full)
    factor = jnp.minimum(1.0, 0.5 * math.sqrt(MODEL_WIDTH * ADAPTER_RANK) / jnp.sqrt(total))
    return (grad_stream.astype(jnp.bfloat16), factor * down_shard, factor * up_full)


def solution(mesh):
    return jax.shard_map(
        local,
        mesh=mesh,
        in_specs=(
            P(("groups", "fsdp", "dp", "pair"), None),
            P(),
            P("fsdp", None),
            P(("groups", "fsdp"), None),
            P("groups", None),
            P(("groups", "fsdp", "dp", "pair"), None),
        ),
        out_specs=(
            P(("groups", "fsdp", "dp", "pair"), None),
            P(("groups", "fsdp"), None),
            P("groups", None),
        ),
        check_vma=False,
    )
```

profile of v0, /device:TPU:0, one launch (start us, length us, event | category | flops | bytes accessed | tf_op | source)
XLA Modules:
  0.0 322.7 jit_solution(588120099054937987)
XLA Ops:
  7.2 0.0 copy-start
  7.2 0.0 reduce-scatter.2.cloned.1.call-start
  7.2 21.6 %all_gather.9 = bf16[512,768]{1,0:T(8,128)(2,1)S(1)} all-gather(bf16[128,768]{1,0:T(8,128)(2,1)} %param.11), channel_id=1, replica_groups=mesh['groups'=2,'fsdp'=4,'dp'=2,'pair'=2] {'fsdp'}, dimensions={0}, use_global_device_ids=true | all-gather | bytes 983040 | tf_op jit(solution)/shard_map/all_gather | solution.py:37
  28.9 1.2 fusion.7
  30.1 12.0 %all_gather.10 = bf16[512,64]{0,1:T(8,128)(2,1)S(1)} all-gather(bf16[128,64]{0,1:T(8,128)(2,1)S(1)} %fusion.7), channel_id=1, replica_groups=mesh['groups'=2,'fsdp'=4,'dp'=2,'pair'=2] {'fsdp'}, dimensions={0}, use_global_device_ids=true | all-gather | bytes 81920 | tf_op jit(solution)/shard_map/all_gather | solution.py:38
  42.1 1.8 fusion.13
  43.9 0.7 add_convert_fusion
  44.6 46.4 %all_to_all.13 = bf16[4,128,2048]{2,1,0:T(8,128)(2,1)S(1)} all-to-all(bf16[4,128,2048]{2,1,0:T(8,128)(2,1)S(1)} %bitcast.16), channel_id=1, replica_groups=mesh['groups'=2,'fsdp'=4,'dp'=2,'pair'=2] {'fsdp'}, dimensions={0} | all-to-all | bytes 4194304 | tf_op jit(solution)/shard_map/all_to_all | solution.py:43
  91.1 0.5 convert_bitcast_fusion
  91.6 0.0 copy-start.2
  91.6 0.5 copy.10
  92.1 1.9 copy-done.1
  94.0 1.2 fusion
  95.2 2.2 fusion.10
  97.4 0.0 reduce-scatter.2.cloned.1.call-update
  97.4 0.0 all-gather.2.cloned.1.call-start
  97.5 0.7 all-gather.2.cloned.1.call-update
  98.2 0.0 all-reduce.3.cloned.1.call-start
  98.2 42.3 %reduce-scatter.2.cloned.1.call-done = f32[2048,64]{0,1:T(8,128)} async-done(((f32[8192,64]{0,1:T(8,128)}), f32[2048,64]{0,1:T(8,128)}) %reduce-scatter.2.cloned.1.call-update) | async-done | bytes 524304 | tf_op jit(solution)/shard_map/reduce_scatter | solution.py:58
  140.5 0.0 all-reduce.3.cloned.1.call-update
  140.6 0.0 all-reduce.5.cloned.1.call-start
  140.6 28.9 %all-gather.2.cloned.1.call-done = bf16[8192,64]{0,1:T(8,128)(2,1)} async-done(((bf16[2048,64]{0,1:T(8,128)(2,1)}), bf16[8192,64]{0,1:T(8,128)(2,1)}) %all-gather.2.cloned.1.call-update) | async-done | bytes 1048592 | tf_op jit(solution)/shard_map/all_gather | solution.py:49
  169.5 3.5 %convolution_multiply_fusion = f32[64,768]{1,0:T(8,128)} fusion(bf16[128,768]{1,0:T(8,128)(2,1)S(1)} %copy-done.4, bf16[8192,64]{0,1:T(8,128)(2,1)} %all-gather.2.cloned.1.call-done, bf16[128,8192]{1,0:T(8,128)(2,1)} %param.6, f32[8192]{0:T(1024)S(1)} %copy-done.5, f32[128]{0:T(128)S(1)} %get-tuple-element.5), kind=kOutput, calls=%fused_computation.13 | convolution fusion | flops 151052288 | bytes 3572224 | tf_op jit(solution)/shard_map/dot_general | solution.py:20
  173.0 0.0 all-reduce.5.cloned.1.call-update
  173.1 5.3 %fusion.3 = bf16[128,8192]{1,0:T(8,128)(2,1)} fusion(bf16[128,8192]{1,0:T(8,128)(2,1)} %param.6, f32[128,8192]{1,0:T(8,128)} %bitcast.15, f32[128]{0:T(128)S(1)} %get-tuple-element.4, f32[128]{0:T(128)S(1)} %get-tuple-element.6, f32[8192]{0:T(1024)S(1)} %copy-done.5, f32[128]{0:T(128)S(1)} %get-tuple-element.5), kind=kLoop, calls=%fused_computation.7 | loop fusion | flops 7340032 | bytes 8422912 | tf_op jit(solution)/shard_map/convert_element_type | solution.py:66
  178.4 26.3 %all-reduce.3.cloned.1.call-done = f32[2048,64]{0,1:T(8,128)} async-done(((f32[2048,64]{0,1:T(8,128)}), f32[2048,64]{0,1:T(8,128)}) %all-reduce.3.cloned.1.call-update) | async-done | bytes 524304 | tf_op jit(solution)/shard_map/psum | solution.py:62
  204.7 1.8 multiply_reduce_fusion
  206.5 92.0 %all-reduce.5.cloned.1.call-done = f32[64,768]{1,0:T(8,128)} async-done(((f32[64,768]{1,0:T(8,128)}), f32[64,768]{1,0:T(8,128)}) %all-reduce.5.cloned.1.call-update) | async-done | bytes 196624 | tf_op jit(solution)/shard_map/psum | solution.py:63
  298.5 1.6 multiply_reduce_fusion.1
  300.1 11.2 %psum.22 = f32[]{:T(128)} all-reduce(f32[]{:T(128)} %multiply_reduce_fusion), channel_id=1, replica_groups=mesh['groups'=2,'fsdp'=4,'dp'=2,'pair'=2] {'fsdp'}, use_global_device_ids=true, to_apply=%region_5.0 | all-reduce | flops 1 | bytes 8 | tf_op jit(solution)/shard_map/psum | solution.py:64
  312.7 1.9 broadcast_multiply_fusion
  314.6 1.6 broadcast_multiply_fusion.1
  (10 shorter events, 0.0 us)
Async XLA Ops:
  7.2 34.9 %copy-start = (bf16[2048,768]{1,0:T(8,128)(2,1)S(1)}, bf16[2048,768]{1,0:T(8,128)(2,1)}, u32[]{:S(2)}) copy-start(bf16[2048,768]{1,0:T(8,128)(2,1)} %param.8) | copy-start | bytes 9437188
  7.2 133.4 %reduce-scatter.2.cloned.1.call-start = ((), (), s32[]{:S(2)}) async-start(), calls=%async_computation.2 | async-start | bytes 2621440 | tf_op jit(solution)/shard_map/reduce_scatter | solution.py:58
  42.1 1.8 copy-start.3
  91.6 2.5 copy-start.2
  91.6 2.4 copy-start.5
  92.1 1.9 copy-start.1
  95.2 74.3 %copy-start.4 = (bf16[128,768]{1,0:T(8,128)(2,1)S(1)}, bf16[128,768]{1,0:T(8,128)(2,1)}, u32[]{:S(2)}) copy-start(bf16[128,768]{1,0:T(8,128)(2,1)} %param.11) | copy-start | bytes 589828
  97.4 72.1 %all-gather.2.cloned.1.call-start = ((), (), s32[]{:S(2)}) async-start(), calls=%async_computation.4 | async-start | bytes 1310720 | tf_op jit(solution)/shard_map/all_gather | solution.py:49
  98.2 106.5 %all-reduce.3.cloned.1.call-start = ((), (), s32[]{:S(2)}) async-start(), calls=%async_computation.3 | async-start | bytes 1048576 | tf_op jit(solution)/shard_map/psum | solution.py:62
  140.6 157.9 %all-reduce.5.cloned.1.call-start = ((), (), s32[]{:S(2)}) async-start(), calls=%async_computation.5 | async-start | bytes 393216 | tf_op jit(solution)/shard_map/psum | solution.py:63
Sparse Core Ops, SparseCore 0:
  97.6 42.9 reduce-scatter.1
  142.2 27.2 all-gather.1
  172.0 32.6 all-reduce.2
  208.9 89.5 all-reduce.4
where the time goes:
time: 323 us
  waiting for transfers between devices  190 us (59%)
  blocking collectives  91.3 us (28%)
  between operations  15.2 us (5%)
  other arithmetic  13.9 us (4%)
  matrix products  9.43 us (3%)
    psum x1, waiting for transfers between devices, local(): up_full = lax.psum(up_portion, ('fsdp', 'dp', 'pair'))  92 us
    all_to_all x1, blocking collectives, local(): lax.all_to_all(columns.astype(jnp.bfloat16), 'fsdp', split_axis=0, concat...  46.4 us
    reduce_scatter x1, waiting for transfers between devices, local(): lax.psum_scatter(contract_leading(window, upward_product), 'fsdp', scatte...  42.3 us
    all_gather x1, waiting for transfers between devices, local(): lax.all_gather(adapter_down_map, 'fsdp', axis=0, tiled=True)  28.9 us
    psum x1, waiting for transfers between devices, local(): down_shard = lax.psum(down_shard, ('dp', 'pair'))  26.3 us
    all_gather x1, blocking collectives, local(): lax.all_gather(values_gradient, 'fsdp', axis=0, tiled=True)  21.6 us
    all_gather x1, blocking collectives, local(): lax.all_gather(upward_product, 'fsdp', axis=0, tiled=True)  12 us
    psum x1, blocking collectives, local(): lax.psum(jnp.sum(down_shard * down_shard), 'fsdp')  11.2 us
  transfers between devices with their start and end apart: 4, of which 4 were waited for; matrix products, arithmetic and copies ran while one was open for 3% of the time, Pallas kernels for 0%

commit v1 on v0

--- a/solution.py
+++ b/solution.py
@@ -8,6 +8,12 @@
 ADAPTER_RANK = 64
 norm_eps = 1e-05
 adapter_scale = 2.0
+
+
+def _save_slabs(local_x):
+    left_arr = lax.psum(local_x, ("dp", "pair"))
+    arr_now = lax.psum(left_arr, "fsdp")
+    return arr_now
 
 
 def contract_last(left, right):
@@ -60,7 +66,7 @@
     )
     up_portion = adapter_scale * contract_leading(latent_code, values_gradient)
     down_shard = lax.psum(down_shard, ("dp", "pair"))
-    up_full = lax.psum(up_portion, ("fsdp", "dp", "pair"))
+    up_full = _save_slabs(up_portion)
     total = lax.psum(jnp.sum(down_shard * down_shard), "fsdp") + jnp.sum(up_full * up_full)
     factor = jnp.minimum(1.0, 0.5 * math.sqrt(MODEL_WIDTH * ADAPTER_RANK) / jnp.sqrt(total))
     return (grad_stream.astype(jnp.bfloat16), factor * down_shard, factor * up_full)

time: 323 us -> 249 us (0.77)
  blocking collectives: 91.3 us -> 46 us
  waiting for transfers between devices: 190 us -> 154 us
  starting transfers between devices: 0.16 us -> 4.6 us
    psum x1, waiting for transfers between devices: 92 us -> 17.6 us  [_save_slabs(): arr_now = lax.psum(left_arr, 'fsdp')]
    all_to_all x0 -> x1, waiting for transfers between devices: none -> 59.7 us  [local(): lax.all_to_all(columns.astype(jnp.bfloat16), 'fsdp', split_axis=0, concat...]
    all_to_all x1 -> x0, blocking collectives: 46.4 us -> none  [local(): lax.all_to_all(columns.astype(jnp.bfloat16), 'fsdp', split_axis=0, concat...]
    all_gather x1, waiting for transfers between devices: 28.9 us -> 0.02 us  [local(): lax.all_gather(adapter_down_map, 'fsdp', axis=0, tiled=True)]
    psum x1, waiting for transfers between devices: 26.3 us -> 36.9 us  [local(): down_shard = lax.psum(down_shard, ('dp', 'pair'))]
    all_to_all x0 -> x1, starting transfers between devices: none -> 4.44 us  [local(): lax.all_to_all(columns.astype(jnp.bfloat16), 'fsdp', split_axis=0, concat...]
  transfers between devices with their start and end apart: 4 -> 5, of which waited for: 4 -> 4; matrix products, arithmetic and copies ran while one was open for 3% -> 6% of each run, Pallas kernels for 0% -> 0%
where the time goes in v1:
time: 249 us
  waiting for transfers between devices  154 us (62%)
  blocking collectives  46 us (18%)
  other arithmetic  15.5 us (6%)
  between operations  15.2 us (6%)
  matrix products  10.8 us (4%)
  starting transfers between devices  4.6 us (2%)
    all_to_all x1, waiting for transfers between devices, local(): lax.all_to_all(columns.astype(jnp.bfloat16), 'fsdp', split_axis=0, concat...  59.7 us
    reduce_scatter x1, waiting for transfers between devices, local(): lax.psum_scatter(contract_leading(window, upward_product), 'fsdp', scatte...  39.5 us
    psum x1, waiting for transfers between devices, local(): down_shard = lax.psum(down_shard, ('dp', 'pair'))  36.9 us
    all_gather x1, blocking collectives, local(): lax.all_gather(values_gradient, 'fsdp', axis=0, tiled=True)  21.6 us
    psum x1, waiting for transfers between devices, _save_slabs(): arr_now = lax.psum(left_arr, 'fsdp')  17.6 us
    psum x1, blocking collectives, local(): lax.psum(jnp.sum(down_shard * down_shard), 'fsdp')  12.4 us
    all_gather x1, blocking collectives, local(): lax.all_gather(upward_product, 'fsdp', axis=0, tiled=True)  12 us
    dot_general x2, matrix products, contract_leading(): lax.dot_general(left, right, (((0,), (0,)), ((), ())), preferred_element_...  5.71 us
  transfers between devices with their start and end apart: 5, of which 4 were waited for; matrix products, arithmetic and copies ran while one was open for 6% of the time, Pallas kernels for 0%

profile of v1, /device:TPU:0, one launch (start us, length us, event | category | flops | bytes accessed | tf_op | source)
XLA Modules:
  0.0 248.9 jit_solution(16437206864968096997)
XLA Ops:
  7.2 0.0 copy-start
  7.2 21.6 %all_gather.9 = bf16[512,768]{1,0:T(8,128)(2,1)S(1)} all-gather(bf16[128,768]{1,0:T(8,128)(2,1)} %param.11), channel_id=1, replica_groups=mesh['groups'=2,'fsdp'=4,'dp'=2,'pair'=2] {'fsdp'}, dimensions={0}, use_global_device_ids=true | all-gather | bytes 983040 | tf_op jit(solution)/shard_map/all_gather | solution.py:43
  28.8 1.2 fusion.7
  30.0 12.0 %all_gather.10 = bf16[512,64]{0,1:T(8,128)(2,1)S(1)} all-gather(bf16[128,64]{0,1:T(8,128)(2,1)S(1)} %fusion.7), channel_id=1, replica_groups=mesh['groups'=2,'fsdp'=4,'dp'=2,'pair'=2] {'fsdp'}, dimensions={0}, use_global_device_ids=true | all-gather | bytes 81920 | tf_op jit(solution)/shard_map/all_gather | solution.py:44
  42.0 1.8 fusion.13
  43.8 2.1 add_convert_fusion
  45.9 4.4 %all-to-all-start = ((bf16[4,128,2048]{2,1,0:T(8,128)(2,1)}), bf16[4,128,2048]{2,1,0:T(8,128)(2,1)}, u32[]{:S(2)}, u32[]{:S(2)}) async-start(bf16[4,128,2048]{2,1,0:T(8,128)(2,1)} %bitcast.16), calls=%async_computation | async-start | bytes 4194304 | tf_op jit(solution)/shard_map/all_to_all | solution.py:49
  50.3 0.0 all-gather.2.cloned.1.call-start
  50.4 0.7 all-gather.2.cloned.1.call-update
  51.1 0.0 reduce-scatter.2.cloned.1.call-start
  51.1 59.7 %all-to-all-done = bf16[4,128,2048]{2,1,0:T(8,128)(2,1)} async-done(((bf16[4,128,2048]{2,1,0:T(8,128)(2,1)}), bf16[4,128,2048]{2,1,0:T(8,128)(2,1)}, u32[]{:S(2)}, u32[]{:S(2)}) %all-to-all-start) | async-done | bytes 2097184 | tf_op jit(solution)/shard_map/all_to_all | solution.py:49
  110.8 2.1 convert_bitcast_fusion
  112.9 0.5 copy.10
  113.4 1.9 copy-done.1
  115.4 1.2 fusion
  116.6 2.2 fusion.10
  118.7 0.0 reduce-scatter.2.cloned.1.call-update
  118.8 0.0 all-reduce.6.cloned.1.call-start
  118.8 0.0 all-gather.2.cloned.1.call-done
  118.9 3.5 %convolution_multiply_fusion = f32[64,768]{1,0:T(8,128)} fusion(bf16[128,768]{1,0:T(8,128)(2,1)S(1)} %copy-done.4, bf16[8192,64]{0,1:T(8,128)(2,1)} %all-gather.2.cloned.1.call-done, bf16[128,8192]{1,0:T(8,128)(2,1)} %param.6, f32[8192]{0:T(1024)S(1)} %copy-done.5, f32[128]{0:T(128)S(1)} %get-tuple-element.7), kind=kOutput, calls=%fused_computation.13 | convolution fusion | flops 151052288 | bytes 3572224 | tf_op jit(solution)/shard_map/dot_general | solution.py:26
  122.4 39.5 %reduce-scatter.2.cloned.1.call-done = f32[2048,64]{0,1:T(8,128)} async-done(((f32[8192,64]{0,1:T(8,128)}), f32[2048,64]{0,1:T(8,128)}) %reduce-scatter.2.cloned.1.call-update) | async-done | bytes 524304 | tf_op jit(solution)/shard_map/reduce_scatter | solution.py:64
  161.9 0.0 all-reduce.6.cloned.1.call-update
  161.9 0.0 all-reduce.4.cloned.1.call-start
  161.9 36.9 %all-reduce.6.cloned.1.call-done = (f32[2048,64]{0,1:T(8,128)}, f32[64,768]{1,0:T(8,128)}) async-done(((f32[2048,64]{0,1:T(8,128)}, f32[64,768]{1,0:T(8,128)}), (f32[2048,64]{0,1:T(8,128)}, f32[64,768]{1,0:T(8,128)})) %all-reduce.6.cloned.1.call-update) | async-done | bytes 720912 | tf_op jit(solution)/shard_map/psum | solution.py:68
  198.8 1.8 multiply_reduce_fusion
  200.6 0.0 all-reduce.4.cloned.1.call-update
  200.6 5.3 %fusion.3 = bf16[128,8192]{1,0:T(8,128)(2,1)} fusion(bf16[128,8192]{1,0:T(8,128)(2,1)} %param.6, f32[128,8192]{1,0:T(8,128)} %bitcast.15, f32[128]{0:T(128)S(1)} %get-tuple-element.4, f32[128]{0:T(128)S(1)} %get-tuple-element.8, f32[8192]{0:T(1024)S(1)} %copy-done.5, f32[128]{0:T(128)S(1)} %get-tuple-element.7), kind=kLoop, calls=%fused_computation.7 | loop fusion | flops 7340032 | bytes 8422912 | tf_op jit(solution)/shard_map/convert_element_type | solution.py:72
  206.0 12.4 %psum.29 = f32[]{:T(128)} all-reduce(f32[]{:T(128)} %multiply_reduce_fusion), channel_id=1, replica_groups=mesh['groups'=2,'fsdp'=4,'dp'=2,'pair'=2] {'fsdp'}, use_global_device_ids=true, to_apply=%region_5.0 | all-reduce | flops 1 | bytes 8 | tf_op jit(solution)/shard_map/psum | solution.py:70
  218.3 17.6 %all-reduce.4.cloned.1.call-done = f32[64,768]{1,0:T(8,128)} async-done(((f32[64,768]{1,0:T(8,128)}), f32[64,768]{1,0:T(8,128)}) %all-reduce.4.cloned.1.call-update) | async-done | bytes 196624 | tf_op jit(solution)/shard_map/psum | solution.py:15
  236.0 1.6 multiply_reduce_fusion.1
  238.9 1.9 broadcast_multiply_fusion
  240.8 1.6 broadcast_multiply_fusion.1
  (11 shorter events, 0.0 us)
Async XLA Ops:
  7.2 34.8 %copy-start = (bf16[2048,768]{1,0:T(8,128)(2,1)S(1)}, bf16[2048,768]{1,0:T(8,128)(2,1)}, u32[]{:S(2)}) copy-start(bf16[2048,768]{1,0:T(8,128)(2,1)} %param.8) | copy-start | bytes 9437188
  42.0 1.8 copy-start.3
  45.9 64.9 %all-to-all-start = ((bf16[4,128,2048]{2,1,0:T(8,128)(2,1)}), bf16[4,128,2048]{2,1,0:T(8,128)(2,1)}, u32[]{:S(2)}, u32[]{:S(2)}) async-start(bf16[4,128,2048]{2,1,0:T(8,128)(2,1)} %bitcast.16), calls=%async_computation | async-start | bytes 4194304 | tf_op jit(solution)/shard_map/all_to_all | solution.py:49
  50.3 68.5 %all-gather.2.cloned.1.call-start = ((), (), s32[]{:S(2)}) async-start(), calls=%async_computation.3 | async-start | bytes 1310720 | tf_op jit(solution)/shard_map/all_gather | solution.py:55
  51.1 110.8 %reduce-scatter.2.cloned.1.call-start = ((), (), s32[]{:S(2)}) async-start(), calls=%async_computation.2 | async-start | bytes 2621440 | tf_op jit(solution)/shard_map/reduce_scatter | solution.py:64
  112.9 2.5 copy-start.2
  112.9 2.5 copy-start.5
  113.4 1.9 copy-start.1
  116.6 2.3 copy-start.4
  118.8 80.1 %all-reduce.6.cloned.1.call-start = ((), (), s32[]{:S(2)}) async-start(), calls=%async_computation.5 | async-start | bytes 1441792 | tf_op jit(solution)/shard_map/psum | solution.py:68
  161.9 74.1 %all-reduce.4.cloned.1.call-start = ((), (), s32[]{:S(2)}) async-start(), calls=%async_computation.4 | async-start | bytes 393216 | tf_op jit(solution)/shard_map/psum | solution.py:15
Sparse Core Ops, SparseCore 0:
  52.8 49.7 all-gather.1
  118.9 42.9 reduce-scatter.1
  165.1 33.6 all-reduce.5
  201.1 34.8 all-reduce.3
